TPU v7x, 512 devices: a whole 4x4x16 slice. The times are simulated.
512 devices in a mesh: dp: 16 (over z), head: 8 (over x, core), srv: 4 (over y).
Axes of the slice: x: 4, y: 4, z: 16, core: 2. Of those that a mesh axis runs over, the one named last changes fastest.
Arguments:
- queries: bfloat16 [2048, 8, 1024], P('dp', 'srv', 'head'), may hold values from -5 to 5
- keys: bfloat16 [10240, 1024], P(('dp', 'head')), may hold values from -5 to 5
- values: bfloat16 [10240, 1024], P(('dp', 'head')), may hold values from -6 to 6
- output_gradient: bfloat16 [2048, 8, 1024], P('dp', 'srv', 'head'), may hold values from -6 to 6
- doc_ids: int32 [10240], P('dp'), may hold values from 0 to 7, never falling along the last dimension, each value on 1 to 5120 neighbouring positions
Outputs:
- attention: bfloat16 [2048, 8, 1024], P('dp', 'srv', 'head')
- q_grad: bfloat16 [2048, 8, 1024], P('dp', 'srv', 'head')
- k_grad: bfloat16 [10240, 1024], P(('dp', 'head', 'srv'))
- v_grad: bfloat16 [10240, 1024], P(('dp', 'head', 'srv'))
Inputs may be any that keep to these rules, and one draw needn't show every extreme that they name: `doc_ids`: document numbers never fall along the keys; every document holds at most 5120 keys, and one holds exactly 5120.
All inputs are finite; a program needn't handle non-finite values.
Results may differ from a plain program's by a relative error of at most 0.039.
Values may be sent and summed in bfloat16 or wider, within the bound.
No kernel may reach another device: no remote copies, remote signals or barrier semaphores. Data moves between devices by JAX's collectives and lax.ppermute only.
A program may use at most 64 MiB of HBM per device.

v0:
```python
import math
import jax
import jax.numpy as jnp
from jax import lax
from jax.sharding import PartitionSpec as P

HEAD_SIZE = 128
NEGATIVE = -1e30


def local(queries, keys, values, output_gradient, doc_ids):
    home_rows, pair_heads, group_width = queries.shape
    groups = group_width // HEAD_SIZE
    scale_factor = HEAD_SIZE ** (-0.5)
    key_rows, value_rows = (
        lax.all_to_all(keys, "head", split_axis=1, concat_axis=0, tiled=True),
        lax.all_to_all(values, "head", split_axis=1, concat_axis=0, tiled=True),
    )
    key_count = key_rows.shape[0]
    servers = lax.axis_size("dp")
    server = lax.axis_index("dp")
    key_at = server * key_count + jnp.arange(key_count, dtype=jnp.int32)
    all_docs = lax.all_gather(doc_ids, "dp", axis=0, tiled=True)
    query_total = home_rows * servers
    context = all_docs.shape[0] - query_total
    query_docs = all_docs[context:]
    query_places = context + jnp.arange(query_total, dtype=jnp.int32)
    all_q, all_dout = (
        lax.all_gather(queries, "dp", axis=0, tiled=True),
        lax.all_gather(output_gradient, "dp", axis=0, tiled=True),
    )
    block_rows = math.gcd(512, query_total)
    block_count = query_total // block_rows
    key_heads = key_rows.reshape(key_count, groups, HEAD_SIZE)
    value_heads = value_rows.reshape(key_count, groups, HEAD_SIZE)
    query_blocks = all_q.reshape(block_count, block_rows, pair_heads, groups, HEAD_SIZE)
    grad_blocks = all_dout.reshape(block_count, block_rows, pair_heads, groups, HEAD_SIZE)
    place_blocks = query_places.reshape(block_count, block_rows)
    doc_blocks = query_docs.reshape(block_count, block_rows)

    def admissible(places, query_doc):
        return (key_at[None, :] <= places[:, None]) & (doc_ids[None, :] == query_doc[:, None])

    def scores_of(query_block):
        return (
            jnp.einsum("pjgd,kgd->gjpk", query_block, key_heads, preferred_element_type=jnp.float32)
            * scale_factor
        )

    def block_max(inputs):
        query_block, places, query_doc = inputs
        allowed = admissible(places, query_doc)

        def compute():
            raw_scores = scores_of(query_block)
            masked = jnp.where(allowed[None, None], raw_scores, NEGATIVE)
            return (jnp.max(masked, axis=-1).transpose(2, 1, 0), raw_scores)

        return compute()

    def block_top(inputs):
        return block_max(inputs)[0]

    local_max = lax.map(block_top, (query_blocks, place_blocks, doc_blocks))
    row_max = lax.pmax(local_max.reshape(query_total, pair_heads, groups), "dp")
    max_blocks = row_max.reshape(block_count, block_rows, pair_heads, groups)

    def block_sum(inputs):
        stored, places, query_doc, row_top = inputs
        allowed = admissible(places, query_doc)

        def compute():
            block_scores = scores_of(stored)
            shifted = block_scores - row_top.transpose(2, 1, 0)[..., None]
            weights = jnp.where(allowed[None, None], jnp.exp(shifted), 0.0)
            weighted = jnp.einsum(
                "gjpk,kgd->pjgd",
                weights.astype(jnp.bfloat16),
                value_heads,
                preferred_element_type=jnp.float32,
            )
            return (
                weighted.reshape(block_rows, pair_heads, group_width),
                jnp.sum(weights, axis=-1).transpose(2, 1, 0),
            )

        return compute()

    part_out, part_norm = lax.map(block_sum, (query_blocks, place_blocks, doc_blocks, max_blocks))
    part_out = part_out.reshape(query_total, pair_heads, group_width)
    part_norm = part_norm.reshape(query_total, pair_heads, groups)
    home_out, home_norm = (
        lax.psum_scatter(part_out, "dp", scatter_dimension=0, tiled=True),
        lax.psum_scatter(part_norm, "dp", scatter_dimension=0, tiled=True),
    )
    home_max = lax.dynamic_slice_in_dim(row_max, server * home_rows, home_rows, 0)
    attn_home = (
        home_out.reshape(home_rows, pair_heads, groups, HEAD_SIZE) / home_norm[..., None]
    ).astype(jnp.bfloat16)
    log_home = home_max + jnp.log(home_norm)
    grad_home = output_gradient.reshape(home_rows, pair_heads, groups, HEAD_SIZE).astype(
        jnp.float32
    )
    delta_home = jnp.sum(grad_home * attn_home.astype(jnp.float32), axis=-1)
    log_all, delta_all = (
        lax.all_gather(log_home, "dp", axis=0, tiled=True),
        lax.all_gather(delta_home, "dp", axis=0, tiled=True),
    )
    attention = attn_home.reshape(home_rows, pair_heads, group_width)
    log_blocks = log_all.reshape(block_count, block_rows, pair_heads, groups)
    delta_blocks = delta_all.reshape(block_count, block_rows, pair_heads, groups)

    def block_grad(totals, inputs):
        query_block, grad_block, places, query_doc, log_norm, row_delta = inputs
        allowed = admissible(places, query_doc)

        def compute():
            shifted = scores_of(query_block) - log_norm.transpose(2, 1, 0)[..., None]
            probs = jnp.where(allowed[None, None], jnp.exp(shifted), 0.0)
            value_grad = jnp.einsum(
                "gjpk,pjgd->kgd",
                probs.astype(jnp.bfloat16),
                grad_block,
                preferred_element_type=jnp.float32,
            )
            weight_grad = jnp.einsum(
                "pjgd,kgd->gjpk", grad_block, value_heads, preferred_element_type=jnp.float32
            )
            score_grad = (probs * (weight_grad - row_delta.transpose(2, 1, 0)[..., None])).astype(
                jnp.bfloat16
            )
            query_grad = (
                jnp.einsum(
                    "gjpk,kgd->pjgd", score_grad, key_heads, preferred_element_type=jnp.float32
                )
                * scale_factor
            )
            key_grad = (
                jnp.einsum(
                    "gjpk,pjgd->kgd", score_grad, query_block, preferred_element_type=jnp.float32
                )
                * scale_factor
            )
            return (query_grad.reshape(block_rows, pair_heads, group_width), key_grad, value_grad)

        query_grad, key_grad, value_grad = compute()
        return ((totals[0] + key_grad, totals[1] + value_grad), query_grad)

    zero_start = jnp.zeros((key_count, groups, HEAD_SIZE), jnp.float32)
    grad_inputs = (query_blocks, grad_blocks, place_blocks, doc_blocks, log_blocks, delta_blocks)
    (key_total, value_total), query_parts = lax.scan(
        block_grad, (zero_start, zero_start), grad_inputs
    )
    q_summed = lax.psum_scatter(
        query_parts.reshape(query_total, pair_heads, group_width).astype(jnp.bfloat16),
        "dp",
        scatter_dimension=0,
        tiled=True,
    )
    spread_key, spread_value = (
        lax.all_to_all(
            key_total.reshape(key_count, group_width).astype(jnp.bfloat16),
            "head",
            split_axis=0,
            concat_axis=1,
            tiled=True,
        ).astype(jnp.float32),
        lax.all_to_all(
            value_total.reshape(key_count, group_width).astype(jnp.bfloat16),
            "head",
            split_axis=0,
            concat_axis=1,
            tiled=True,
        ).astype(jnp.float32),
    )
    k_summed, v_summed = (
        lax.psum_scatter(
            spread_key.astype(jnp.bfloat16), "srv", scatter_dimension=0, tiled=True
        ).astype(jnp.float32),
        lax.psum_scatter(
            spread_value.astype(jnp.bfloat16), "srv", scatter_dimension=0, tiled=True
        ).astype(jnp.float32),
    )
    return (attention, q_summed, k_summed.astype(jnp.bfloat16), v_summed.astype(jnp.bfloat16))


def solution(mesh):
    placed = (
        P("dp", "srv", "head"),
        P(("dp", "head"), None),
        P(("dp", "head"), None),
        P("dp", "srv", "head"),
        P("dp"),
    )
    return jax.shard_map(
        local,
        mesh=mesh,
        in_specs=placed,
        out_specs=(
            P("dp", "srv", "head"),
            P("dp", "srv", "head"),
            P(("dp", "head", "srv"), None),
            P(("dp", "head", "srv"), None),
        ),
        check_vma=False,
    )
```

profile of v0, /device:TPU:2, one launch (start us, length us, event | category | flops | bytes accessed | tf_op | source)
XLA Modules:
  0.0 651.0 jit_solution(6897663471784736279)
XLA Ops:
  7.2 1.5 copy.61
  9.5 9.2 %all-to-all-start = ((bf16[80,8,128]{2,0,1:T(8,128)(2,1)}), bf16[80,8,128]{2,0,1:T(8,128)(2,1)S(1)}, u32[]{:S(2)}, u32[]{:S(2)}) async-start(bf16[80,8,128]{2,0,1:T(8,128)(2,1)} %copy_bitcast_fusion.3), calls=%async_computation | async-start | bytes 327680 | tf_op jit(solution)/shard_map/all_to_all | solution.py:16
  18.7 1.6 copy_bitcast_fusion.2
  21.0 31.2 %all-gather.1 = s32[16,1,640]{2,1,0:T(1,128)S(1)} all-gather(s32[1,1,640]{2,1,0:T(1,128)S(1)} %reshape.364), channel_id=1, replica_groups=mesh['dp'=16,'head'=8,'srv'=4] {'dp'}, dimensions={0}, use_global_device_ids=true | all-gather | bytes 43520 | tf_op jit(solution)/shard_map/all_gather | solution.py:23
  52.8 33.4 %all-gather.5.cloned.1.call-done = bf16[2048,2,128]{2,0,1:T(8,128)(2,1)} async-done(((bf16[128,2,128]{2,0,1:T(8,128)(2,1)}), bf16[2048,2,128]{2,0,1:T(8,128)(2,1)}) %all-gather.5.cloned.1.call-update) | async-done | bytes 1048592 | tf_op jit(solution)/shard_map/all_gather | solution.py:29
  86.3 1.3 copy.66
  87.6 4.8 all-to-all-start.1
  92.4 7.6 %while.39 = (s32[]{:T(128)}, f32[4,512,2,1]{1,0,2,3:T(4,128)S(1)}, s32[4,512]{1,0:T(4,128)}, s32[640]{0:T(1024)S(1)}, s32[4,512]{1,0:T(4,128)S(1)}, /*index=5*/b...) while((s32[]{:T(128)}, f32[4,512,2,1]{1,0,2,3:T(4,128)S(1)}, ...), condition=%wide.region_2.3_spmd.clone, body=%wide.region_0.2_spmd.clone.sunk | while | flops 170720896 | bytes 1121917 | solution.py:64
  92.4 0.7 constant_dynamic-slice_fusion.12
  93.5 0.8 fusion.104
  94.3 0.7 constant_dynamic-slice_fusion.12
  95.4 0.8 fusion.104
  96.2 0.7 constant_dynamic-slice_fusion.12
  97.3 0.8 fusion.104
  99.2 0.8 fusion.104
  100.0 55.1 %pmax.7 = f32[2048,2,1]{0,1,2:T(2,128)} all-reduce(f32[2048,2,1]{0,1,2:T(2,128)S(1)} %reshape.354), channel_id=1, replica_groups=mesh['dp'=16,'head'=8,'srv'=4] {'dp'}, use_global_device_ids=true, to_apply=%region_3.4 | all-reduce | flops 4096 | bytes 32768 | tf_op jit(solution)/shard_map/pmax | solution.py:65
  155.1 22.3 %while.40 = (s32[]{:T(128)}, f32[4,512,2,128]{3,2,1,0:T(2,128)S(1)}, f32[4,512,2,1]{1,3,2,0:T(1,128)}, s32[4,512]{1,0:T(4,128)}, s32[640]{0:T(1024)S(1)}, /*inde...) while((s32[]{:T(128)}, ...), condition=%wide.region_6.7_spmd.clone, body=%wide.region_4.6_spmd.clone.sunk | while | flops 341769856 | bytes 8437397 | solution.py:89
  156.9 1.1 fusion.107
  157.9 1.7 fusion.108
  162.4 1.0 fusion.107
  163.5 1.7 fusion.108
  168.0 1.0 fusion.107
  169.1 1.7 fusion.108
  173.6 1.0 fusion.107
  174.6 1.7 fusion.108
  177.4 2.1 copy.88
  181.1 1.3 dynamic-slice
  183.0 63.6 %reduce-scatter.8.cloned.1.call-done = f32[128,2]{1,0:T(8,128)} async-done(((f32[2048,2]{1,0:T(8,128)}), f32[128,2]{1,0:T(8,128)}) %reduce-scatter.8.cloned.1.call-update) | async-done | bytes 1040
  246.6 0.9 copy.87
  248.3 27.4 %all_gather.17 = f32[2048,2,1]{0,1,2:T(2,128)S(1)} all-gather(f32[128,2,1]{0,1,2:T(2,128)S(1)} %log_add_fusion), channel_id=1, replica_groups=mesh['dp'=16,'head'=8,'srv'=4] {'dp'}, dimensions={0}, use_global_device_ids=true | all-gather | bytes 17408 | tf_op jit(solution)/shard_map/all_gather | solution.py:106
  275.7 115.2 %all-reduce.10.cloned.1.call-done = f32[2048,2,128]{2,1,0:T(2,128)} async-done(((f32[2048,2,128]{2,1,0:T(2,128)}), f32[2048,2,128]{2,1,0:T(2,128)}) %all-reduce.10.cloned.1.call-update) | async-done | bytes 2097168
  390.9 1.7 multiply_reduce_fusion
  392.6 35.8 %all-gather = f32[2048,2]{1,0:T(8,128)S(1)} all-gather(f32[128,2]{1,0:T(8,128)S(1)} %get-tuple-element.445), channel_id=2, replica_groups=mesh['dp'=16,'head'=8,'srv'=4] {'dp'}, dimensions={0}, use_global_device_ids=true | all-gather | bytes 17408 | tf_op jit(solution)/shard_map/all_gather | solution.py:107
  428.7 32.1 %all-gather.7.cloned.1.call-done = bf16[2048,2,128]{2,0,1:T(8,128)(2,1)} async-done(((bf16[128,2,128]{2,0,1:T(8,128)(2,1)}), bf16[2048,2,128]{2,0,1:T(8,128)(2,1)}) %all-gather.7.cloned.1.call-update) | async-done | bytes 1048592 | tf_op jit(solution)/shard_map/all_gather | solution.py:30
  460.8 37.4 %while.41 = (s32[]{:T(128)}, f32[640,1,128]{0,2,1:T(8,128)S(1)}, f32[640,1,128]{0,2,1:T(8,128)}, bf16[4,512,2,128]{3,1,2,0:T(8,128)(2,1)}, bf16[4,512,2,1,128]{4...) while((s32[]{:T(128)}, f32[640,1,128]{0,2,1:T(8,128)S(1)}, ...), condition=%wide.region_11.12_spmd.clone, body=%wide.region_10.11_spmd.clone.sunk | while | flops 846938752 | bytes 35077916 | solution.py:151
  461.4 0.8 constant_dynamic-slice_fusion.14
  462.5 2.0 fusion.120
  465.0 3.6 fusion.122
  469.2 1.0 copy-done.5
  470.7 0.8 constant_dynamic-slice_fusion.14
  471.8 2.0 fusion.120
  474.4 3.6 fusion.122
  478.5 1.0 copy-done.5
  480.1 0.8 constant_dynamic-slice_fusion.14
  481.1 2.0 fusion.120
  483.7 3.6 fusion.122
  487.9 1.0 copy-done.5
  489.4 0.8 constant_dynamic-slice_fusion.14
  490.5 2.0 fusion.120
  493.1 3.6 fusion.122
  497.2 1.0 copy-done.5
  498.2 0.8 copy.78
  499.0 4.9 all-to-all-start.2
  503.9 3.3 copy.77
  507.2 0.8 copy.80
  508.0 0.9 all-to-all-done.2
  508.9 4.8 all-to-all-start.3
  513.7 5.0 all-to-all-done.3
  518.8 12.6 %fusion.72 = (bf16[24,1024]{1,0:T(8,128)(2,1)S(1)}, bf16[24,1024]{1,0:T(8,128)(2,1)S(1)}) fusion(bf16[80,1024]{1,0:T(8,128)(2,1)S(1)} %copy_bitcast_fusion.1, bf16[80,1024]{1,0:T(8,128)(2,1)S(1)} %copy_bitcast_fusion), kind=kCustom, calls=%all-reduce-scatter.2 | all-reduce-scatter fusion | flops 196609 | bytes 428032
  531.4 1.6 collective-permute-start
  533.0 3.1 collective-permute-start.1
  536.0 1.3 dynamic-slice.10
  539.6 103.4 %all-reduce.12.cloned.1.call-done = bf16[2048,2,128]{2,1,0:T(2,128)(2,1)} async-done(((bf16[2048,2,128]{2,1,0:T(2,128)(2,1)}), bf16[2048,2,128]{2,1,0:T(2,128)(2,1)}) %all-reduce.12.cloned.1.call-update) | async-done | bytes 1048592
  643.0 1.5 constant_dynamic-slice_fusion.8
  (133 shorter events, 27.3 us)
Async XLA Ops:
  7.2 1.6 copy-start
  7.2 85.2 %copy-start.3 = (s32[640]{0:T(1024)S(1)}, s32[640]{0:T(1024)}, u32[]{:S(2)}) copy-start(s32[640]{0:T(1024)} %param.15) | copy-start | bytes 7684
  7.2 79.1 %all-gather.5.cloned.1.call-start = ((), (), s32[]{:S(2)}) async-start(), calls=%async_computation.5 | async-start | bytes 1114112 | tf_op jit(solution)/shard_map/all_gather | solution.py:29
  9.5 78.1 %all-to-all-start = ((bf16[80,8,128]{2,0,1:T(8,128)(2,1)}), bf16[80,8,128]{2,0,1:T(8,128)(2,1)S(1)}, u32[]{:S(2)}, u32[]{:S(2)}) async-start(bf16[80,8,128]{2,0,1:T(8,128)(2,1)} %copy_bitcast_fusion.3), calls=%async_computation | async-start | bytes 327680 | tf_op jit(solution)/shard_map/all_to_all | solution.py:16
  87.6 67.6 %all-to-all-start.1 = ((bf16[80,8,128]{2,0,1:T(8,128)(2,1)}), bf16[80,8,128]{2,0,1:T(8,128)(2,1)}, u32[]{:S(2)}, u32[]{:S(2)}) async-start(bf16[80,8,128]{2,0,1:T(8,128)(2,1)} %copy_bitcast_fusion.2), calls=%async_computation.1 | async-start | bytes 327680 | tf_op jit(solution)/shard_map/all_to_all | solution.py:17
  92.4 154.2 %reduce-scatter.8.cloned.1.call-start = ((), (), s32[]{:S(2)}) async-start(), calls=%async_computation.7 | async-start | bytes 1114112
  177.4 2.2 copy-start.2
  177.4 2.9 copy-start.7
  179.6 211.3 %all-reduce.10.cloned.1.call-start = ((), (), s32[]{:S(2)}) async-start(), calls=%async_computation.8 | async-start | bytes 4194304
  180.3 280.5 %all-gather.7.cloned.1.call-start = ((), (), s32[]{:S(2)}) async-start(), calls=%async_computation.6 | async-start | bytes 1114112 | tf_op jit(solution)/shard_map/all_gather | solution.py:30
  461.3 3.2 copy-start.1
  465.0 3.6 copy-start.4
  469.2 1.0 copy-start.5
  470.7 3.2 copy-start.1
  474.4 3.6 copy-start.4
  478.5 1.0 copy-start.5
  480.0 3.2 copy-start.1
  483.7 3.6 copy-start.4
  487.9 1.0 copy-start.5
  489.4 3.2 copy-start.1
  493.1 3.6 copy-start.4
  497.2 1.0 copy-start.5
  498.2 9.0 %copy-start.6 = (f32[640,1,128]{0,2,1:T(8,128)S(1)}, f32[640,1,128]{0,2,1:T(8,128)}, u32[]{:S(2)}) copy-start(f32[640,1,128]{0,2,1:T(8,128)} %get-tuple-element.183) | copy-start | bytes 983044
  499.0 9.9 %all-to-all-start.2 = ((bf16[8,80,128]{2,1,0:T(8,128)(2,1)}), bf16[8,80,128]{2,1,0:T(8,128)(2,1)S(1)}, u32[]{:S(2)}, u32[]{:S(2)}) async-start(bf16[8,80,128]{2,1,0:T(8,128)(2,1)} %bitcast.15), calls=%async_computation.2 | async-start | bytes 327680 | tf_op jit(solution)/shard_map/all_to_all | solution.py:161
  503.9 139.1 %all-reduce.12.cloned.1.call-start = ((), (), s32[]{:S(2)}) async-start(), calls=%async_computation.9 | async-start | bytes 2097152
  508.9 9.8 %all-to-all-start.3 = ((bf16[8,80,128]{2,1,0:T(8,128)(2,1)}), bf16[8,80,128]{2,1,0:T(8,128)(2,1)S(1)}, u32[]{:S(2)}, u32[]{:S(2)}) async-start(bf16[8,80,128]{2,1,0:T(8,128)(2,1)} %bitcast.17), calls=%async_computation.3 | async-start | bytes 327680 | tf_op jit(solution)/shard_map/all_to_all | solution.py:168
  531.4 6.6 %collective-permute-start = (bf16[12,1024]{1,0:T(8,128)(2,1)S(1)}, bf16[12,1024]{1,0:T(8,128)(2,1)S(1)}, u32[]{:S(2)}, u32[]{:S(2)}) collective-permute-start(bf16[12,1024]{1,0:T(8,128)(2,1)S(1)} %slice.16), channel_id=1, source_target_pairs={{0,1},{1,2},{2,3},{4,5},{5,6},{6,7},{8,9},{9,10},{10,11},{12,13},{... | collective-permute-start | bytes 73736
  533.0 5.2 collective-permute-start.1
Sparse Core Ops, SparseCore 0:
  10.7 75.5 all-gather.4
  179.7 66.8 reduce-scatter.7
  249.1 141.7 all-reduce.9
  393.6 67.1 all-gather.6
  507.3 135.5 all-reduce.11
where the time goes:
time: 653 us; the launch traced here: 651 us
  waiting for transfers between devices  354 us (54%)
  blocking collectives  162 us (25%)
  matrix products  42.8 us (7%)
  local copies, waits for them, and re-layouts  40.5 us (6%)
  starting transfers between devices  28.4 us (4%)
  between operations  15.3 us (2%)
  other arithmetic  7 us (1%)
    unnamed x10, waiting for transfers between devices  283 us
    pmax x1, blocking collectives, local(): row_max = lax.pmax(local_max.reshape(query_total, pair_heads, groups), 'dp')  55.1 us
    all_gather x1, blocking collectives, local(): lax.all_gather(delta_home, 'dp', axis=0, tiled=True)  35.8 us
    all_gather x1, waiting for transfers between devices, local(): lax.all_gather(queries, 'dp', axis=0, tiled=True)  33.4 us
    all_gather x1, waiting for transfers between devices, local(): lax.all_gather(output_gradient, 'dp', axis=0, tiled=True)  32.1 us
    all_gather x1, blocking collectives, local(): all_docs = lax.all_gather(doc_ids, 'dp', axis=0, tiled=True)  31.2 us
    all_gather x1, blocking collectives, local(): lax.all_gather(log_home, 'dp', axis=0, tiled=True)  27.4 us
    dot_general x4, matrix products, compute(): jnp.einsum('gjpk,pjgd->kgd', probs.astype(jnp.bfloat16), grad_block, pref...  14.3 us
  transfers between devices with their start and end apart: 11, of which 7 were waited for; matrix products, arithmetic and copies ran while one was open for 6% of the time, Pallas kernels for 0%

commit v1 on v0

--- a/solution.py
+++ b/solution.py
@@ -8,7 +8,37 @@
 NEGATIVE = -1e30
 
 
+def work_panel(message, dim_i):
+    message = jnp.moveaxis(message, 0, dim_i)
+    y_new = message.shape
+    return message.reshape(*y_new[:dim_i], y_new[dim_i] * y_new[dim_i + 1], *y_new[dim_i + 2 :])
+
+
 def local(queries, keys, values, output_gradient, doc_ids):
+
+    def forms_play(dim_k, link_axis, field):
+        kept_rows = []
+        amount_of = lax.axis_size(link_axis)
+        for u in range(amount_of):
+            kept_rows.append((u, (u + 1) % amount_of))
+        rack = []
+        for m, jj in kept_rows:
+            rack.append((jj, m))
+        new, piece_out = ([], [])
+        for j0 in range(amount_of - 1):
+            if j0 % 2 == 0:
+                b_next = lax.ppermute(new[-1] if new else field, link_axis, kept_rows)
+                new.append(b_next)
+            else:
+                raw_out = lax.ppermute(piece_out[-1] if piece_out else field, link_axis, rack)
+                piece_out.append(raw_out)
+        p_next = jnp.stack([*new[::-1], field, *piece_out], 0)
+        tmp = lax.axis_index(link_axis)
+        heard = len(new)
+        prior = tmp - heard
+        p_next = p_next[(jnp.arange(amount_of) - prior) % amount_of]
+        return work_panel(p_next, dim_k)
+
     home_rows, pair_heads, group_width = queries.shape
     groups = group_width // HEAD_SIZE
     scale_factor = HEAD_SIZE ** (-0.5)
@@ -104,7 +134,7 @@
     delta_home = jnp.sum(grad_home * attn_home.astype(jnp.float32), axis=-1)
     log_all, delta_all = (
         lax.all_gather(log_home, "dp", axis=0, tiled=True),
-        lax.all_gather(delta_home, "dp", axis=0, tiled=True),
+        forms_play(0, "dp", delta_home),
     )
     attention = attn_home.reshape(home_rows, pair_heads, group_width)
     log_blocks = log_all.reshape(block_count, block_rows, pair_heads, groups)

time: 653 us -> 677 us (1.037)
  starting transfers between devices: 28.4 us -> 77.6 us
  blocking collectives: 162 us -> 128 us
  waiting for transfers between devices: 354 us -> 362 us
    ppermute x0 -> x15, starting transfers between devices: none -> 49.3 us  [the longest x7 32.7 us: forms_play(): lax.ppermute(piece_out[-1] if piece_out else field, link_axis, rack)]
    all_gather x1 -> x0, blocking collectives: 35.8 us -> none  [local(): lax.all_gather(delta_home, 'dp', axis=0, tiled=True)]
    unnamed x10, waiting for transfers between devices: 283 us -> 312 us
    all_gather x1, waiting for transfers between devices: 32.1 us -> 3.58 us  [local(): lax.all_gather(output_gradient, 'dp', axis=0, tiled=True)]
    ppermute x0 -> x15, waiting for transfers between devices: none -> 6.87 us  [the longest x8 3.51 us: forms_play(): b_next = lax.ppermute(new[-1] if new else field, link_axis, kept_rows)]
  transfers between devices with their start and end apart: 11 -> 26, of which waited for: 7 -> 9; matrix products, arithmetic and copies ran while one was open for 6% -> 5% of each run, Pallas kernels for 0% -> 0%
where the time goes in v1:
time: 677 us; the launch traced here: 675 us
  waiting for transfers between devices  362 us (53%)
  blocking collectives  128 us (19%)
  starting transfers between devices  77.6 us (11%)
  matrix products  42.9 us (6%)
  local copies, waits for them, and re-layouts  40.9 us (6%)
  between operations  15.5 us (2%)
  other arithmetic  7.02 us (1%)
    unnamed x10, waiting for transfers between devices  312 us
    pmax x1, blocking collectives, local(): row_max = lax.pmax(local_max.reshape(query_total, pair_heads, groups), 'dp')  55.1 us
    all_gather x1, waiting for transfers between devices, local(): lax.all_gather(queries, 'dp', axis=0, tiled=True)  33.4 us
    ppermute x7, starting transfers between devices, forms_play(): lax.ppermute(piece_out[-1] if piece_out else field, link_axis, rack)  32.7 us
    all_gather x1, blocking collectives, local(): all_docs = lax.all_gather(doc_ids, 'dp', axis=0, tiled=True)  31.2 us
    all_gather x1, blocking collectives, local(): lax.all_gather(log_home, 'dp', axis=0, tiled=True)  29.2 us
    ppermute x8, starting transfers between devices, forms_play(): b_next = lax.ppermute(new[-1] if new else field, link_axis, kept_rows)  16.7 us
    dot_general x4, matrix products, compute(): jnp.einsum('gjpk,pjgd->kgd', probs.astype(jnp.bfloat16), grad_block, pref...  14.3 us
  transfers between devices with their start and end apart: 26, of which 9 were waited for; matrix products, arithmetic and copies ran while one was open for 5% of the time, Pallas kernels for 0%

profile of v1, /device:TPU:2, one launch (start us, length us, event | category | flops | bytes accessed | tf_op | source)
XLA Modules:
  0.0 674.6 jit_solution(462577911891509067)
XLA Ops:
  7.2 1.5 copy.77
  9.5 9.2 %all-to-all-start = ((bf16[80,8,128]{2,0,1:T(8,128)(2,1)}), bf16[80,8,128]{2,0,1:T(8,128)(2,1)S(1)}, u32[]{:S(2)}, u32[]{:S(2)}) async-start(bf16[80,8,128]{2,0,1:T(8,128)(2,1)} %copy_bitcast_fusion.3), calls=%async_computation | async-start | bytes 327680 | tf_op jit(solution)/shard_map/all_to_all | solution.py:46
  18.7 1.6 copy_bitcast_fusion.2
  21.0 31.2 %all-gather = s32[16,1,640]{2,1,0:T(1,128)S(1)} all-gather(s32[1,1,640]{2,1,0:T(1,128)S(1)} %reshape.419), channel_id=1, replica_groups=mesh['dp'=16,'head'=8,'srv'=4] {'dp'}, dimensions={0}, use_global_device_ids=true | all-gather | bytes 43520 | tf_op jit(solution)/shard_map/all_gather | solution.py:53
  52.8 33.4 %all-gather.4.cloned.1.call-done = bf16[2048,2,128]{2,0,1:T(8,128)(2,1)} async-done(((bf16[128,2,128]{2,0,1:T(8,128)(2,1)}), bf16[2048,2,128]{2,0,1:T(8,128)(2,1)}) %all-gather.4.cloned.1.call-update) | async-done | bytes 1048592 | tf_op jit(solution)/shard_map/all_gather | solution.py:59
  86.3 1.3 copy.82
  87.6 4.8 all-to-all-start.1
  92.4 7.6 %while.39 = (s32[]{:T(128)}, f32[4,512,2,1]{1,0,2,3:T(4,128)S(1)}, s32[4,512]{1,0:T(4,128)}, s32[640]{0:T(1024)S(1)}, s32[4,512]{1,0:T(4,128)S(1)}, /*index=5*/b...) while((s32[]{:T(128)}, f32[4,512,2,1]{1,0,2,3:T(4,128)S(1)}, ...), condition=%wide.region_2.3_spmd.clone, body=%wide.region_0.2_spmd.clone.sunk | while | flops 170720896 | bytes 1121917 | solution.py:94
  100.0 55.1 %pmax.7 = f32[2048,2,1]{0,1,2:T(2,128)} all-reduce(f32[2048,2,1]{0,1,2:T(2,128)S(1)} %reshape.401), channel_id=1, replica_groups=mesh['dp'=16,'head'=8,'srv'=4] {'dp'}, use_global_device_ids=true, to_apply=%region_3.4 | all-reduce | flops 4096 | bytes 32768 | tf_op jit(solution)/shard_map/pmax | solution.py:95
  155.1 22.3 %while.40 = (s32[]{:T(128)}, f32[4,512,2,128]{3,2,1,0:T(2,128)S(1)}, f32[4,512,2,1]{1,3,2,0:T(1,128)}, s32[4,512]{1,0:T(4,128)}, s32[640]{0:T(1024)S(1)}, /*inde...) while((s32[]{:T(128)}, ...), condition=%wide.region_6.7_spmd.clone, body=%wide.region_4.6_spmd.clone.sunk | while | flops 341769856 | bytes 8437397 | solution.py:119
  156.9 1.1 fusion.109
  157.9 1.7 fusion.110
  162.4 1.0 fusion.109
  163.5 1.7 fusion.110
  168.0 1.0 fusion.109
  169.1 1.7 fusion.110
  173.6 1.0 fusion.109
  174.6 1.7 fusion.110
  177.4 2.2 copy.118
  180.4 1.3 dynamic-slice
  182.4 64.3 %reduce-scatter.8.cloned.1.call-done = f32[128,2]{1,0:T(8,128)} async-done(((f32[2048,2]{1,0:T(8,128)}), f32[128,2]{1,0:T(8,128)}) %reduce-scatter.8.cloned.1.call-update) | async-done | bytes 1040
  247.7 143.4 %all-reduce.10.cloned.1.call-done = f32[2048,2,128]{2,1,0:T(2,128)} async-done(((f32[2048,2,128]{2,1,0:T(2,128)}), f32[2048,2,128]{2,1,0:T(2,128)}) %all-reduce.10.cloned.1.call-update) | async-done | bytes 2097168
  391.1 1.8 multiply_reduce_fusion
  392.9 3.2 collective-permute-start
  396.1 3.5 collective-permute-done
  399.6 1.9 collective-permute-start.1
  401.6 5.1 collective-permute-start.8
  406.7 1.9 collective-permute-start.2
  408.6 5.1 collective-permute-start.9
  413.8 1.9 collective-permute-start.3
  416.4 5.1 collective-permute-start.10
  421.5 1.9 collective-permute-start.4
  423.5 5.1 collective-permute-start.11
  428.6 1.9 collective-permute-start.5
  430.6 5.1 collective-permute-start.12
  435.8 1.9 collective-permute-start.6
  438.4 5.1 collective-permute-start.13
  443.5 1.9 collective-permute-start.7
  445.5 29.2 %all_gather.14 = f32[2048,2,1]{0,1,2:T(2,128)S(1)} all-gather(f32[128,2,1]{0,1,2:T(2,128)S(1)} %log_add_fusion), channel_id=1, replica_groups=mesh['dp'=16,'head'=8,'srv'=4] {'dp'}, dimensions={0}, use_global_device_ids=true | all-gather | bytes 17408 | tf_op jit(solution)/shard_map/all_gather | solution.py:136
  474.6 1.9 collective-permute-start.14
  476.7 3.3 collective-permute-done.14
  480.7 3.6 all-gather.6.cloned.1.call-done
  484.3 37.3 %while.41 = (s32[]{:T(128)}, f32[640,1,128]{0,2,1:T(8,128)S(1)}, f32[640,1,128]{0,2,1:T(8,128)}, bf16[4,512,2,128]{3,1,2,0:T(8,128)(2,1)}, bf16[4,512,2,1,128]{4...) while((s32[]{:T(128)}, f32[640,1,128]{0,2,1:T(8,128)S(1)}, ...), condition=%wide.region_11.12_spmd.clone, body=%wide.region_10.11_spmd.clone.sunk | while | flops 846938752 | bytes 35077916 | solution.py:181
  485.9 2.0 fusion.122
  488.5 3.6 fusion.124
  492.6 1.0 copy-done.5
  495.2 2.0 fusion.122
  497.8 3.6 fusion.124
  501.9 1.0 copy-done.5
  504.5 2.0 fusion.122
  507.1 3.6 fusion.124
  511.3 1.0 copy-done.5
  513.9 2.0 fusion.122
  516.5 3.6 fusion.124
  522.4 4.8 all-to-all-start.2
  527.2 3.3 copy.109
  532.2 4.8 all-to-all-start.3
  537.0 5.0 all-to-all-done.3
  542.1 12.7 %fusion.74 = (bf16[24,1024]{1,0:T(8,128)(2,1)S(1)}, bf16[24,1024]{1,0:T(8,128)(2,1)S(1)}) fusion(bf16[80,1024]{1,0:T(8,128)(2,1)S(1)} %copy_bitcast_fusion.1, bf16[80,1024]{1,0:T(8,128)(2,1)S(1)} %copy_bitcast_fusion), kind=kCustom, calls=%all-reduce-scatter.2 | all-reduce-scatter fusion | flops 196609 | bytes 428032
  554.8 1.5 collective-permute-start.15
  556.3 3.1 collective-permute-start.16
  559.5 1.3 dynamic-slice.10
  563.0 103.6 %all-reduce.12.cloned.1.call-done = bf16[2048,2,128]{2,1,0:T(2,128)(2,1)} async-done(((bf16[2048,2,128]{2,1,0:T(2,128)(2,1)}), bf16[2048,2,128]{2,1,0:T(2,128)(2,1)}) %all-reduce.12.cloned.1.call-update) | async-done | bytes 1048592
  666.6 1.5 constant_dynamic-slice_fusion.8
  (181 shorter events, 40.4 us)
Async XLA Ops:
  7.2 1.6 copy-start
  7.2 85.2 %copy-start.3 = (s32[640]{0:T(1024)S(1)}, s32[640]{0:T(1024)}, u32[]{:S(2)}) copy-start(s32[640]{0:T(1024)} %param.15) | copy-start | bytes 7684
  7.2 79.1 %all-gather.4.cloned.1.call-start = ((), (), s32[]{:S(2)}) async-start(), calls=%async_computation.5 | async-start | bytes 1114112 | tf_op jit(solution)/shard_map/all_gather | solution.py:59
  9.5 78.1 %all-to-all-start = ((bf16[80,8,128]{2,0,1:T(8,128)(2,1)}), bf16[80,8,128]{2,0,1:T(8,128)(2,1)S(1)}, u32[]{:S(2)}, u32[]{:S(2)}) async-start(bf16[80,8,128]{2,0,1:T(8,128)(2,1)} %copy_bitcast_fusion.3), calls=%async_computation | async-start | bytes 327680 | tf_op jit(solution)/shard_map/all_to_all | solution.py:46
  87.6 67.6 %all-to-all-start.1 = ((bf16[80,8,128]{2,0,1:T(8,128)(2,1)}), bf16[80,8,128]{2,0,1:T(8,128)(2,1)}, u32[]{:S(2)}, u32[]{:S(2)}) async-start(bf16[80,8,128]{2,0,1:T(8,128)(2,1)} %copy_bitcast_fusion.2), calls=%async_computation.1 | async-start | bytes 327680 | tf_op jit(solution)/shard_map/all_to_all | solution.py:47
  92.4 154.3 %reduce-scatter.8.cloned.1.call-start = ((), (), s32[]{:S(2)}) async-start(), calls=%async_computation.7 | async-start | bytes 1114112
  177.4 2.3 copy-start.2
  177.4 213.7 %copy-start.7 = (bf16[128,2,128]{2,1,0:T(2,128)(2,1)S(1)}, bf16[128,2,128]{2,1,0:T(2,128)(2,1)}, u32[]{:S(2)}) copy-start(bf16[128,2,128]{2,1,0:T(2,128)(2,1)} %param.14) | copy-start | bytes 196612
  179.7 211.5 %all-reduce.10.cloned.1.call-start = ((), (), s32[]{:S(2)}) async-start(), calls=%async_computation.8 | async-start | bytes 4194304
  180.4 303.9 %all-gather.6.cloned.1.call-start = ((), (), s32[]{:S(2)}) async-start(), calls=%async_computation.6 | async-start | bytes 1114112 | tf_op jit(solution)/shard_map/all_gather | solution.py:60
  392.9 6.7 collective-permute-start
  399.6 7.1 %collective-permute-start.1 = (f32[128,2,1]{0,1,2:T(2,128)S(1)}, f32[128,2,1]{0,1,2:T(2,128)S(1)}, u32[]{:S(2)}, u32[]{:S(2)}) collective-permute-start(f32[128,2,1]{0,1,2:T(2,128)S(1)} %collective-permute-done), channel_id=1, source_target_pairs={{0,32},{32,64},{64,96},{96,128},{128,160},{160,192},{192,224},{224... | collective-permute-start | bytes 3080 | tf_op jit(solution)/shard_map/ppermute | solution.py:30
  401.6 7.0 %collective-permute-start.8 = (f32[128,2,1]{0,1,2:T(2,128)S(1)}, f32[128,2,1]{0,1,2:T(2,128)S(1)}, u32[]{:S(2)}, u32[]{:S(2)}) collective-permute-start(f32[128,2,1]{0,1,2:T(2,128)S(1)} %bitcast.410), channel_id=1, source_target_pairs={{32,0},{64,32},{96,64},{128,96},{160,128},{192,160},{224,192},{256... | collective-permute-start | bytes 3080 | tf_op jit(solution)/shard_map/ppermute | solution.py:33
  406.7 7.1 %collective-permute-start.2 = (f32[128,2,1]{0,1,2:T(2,128)S(1)}, f32[128,2,1]{0,1,2:T(2,128)S(1)}, u32[]{:S(2)}, u32[]{:S(2)}) collective-permute-start(f32[128,2,1]{0,1,2:T(2,128)S(1)} %collective-permute-done.1), channel_id=1, source_target_pairs={{0,32},{32,64},{64,96},{96,128},{128,160},{160,192},{192,224},{224... | collective-permute-start | bytes 3080 | tf_op jit(solution)/shard_map/ppermute | solution.py:30
  408.6 7.8 %collective-permute-start.9 = (f32[128,2,1]{0,1,2:T(2,128)S(1)}, f32[128,2,1]{0,1,2:T(2,128)S(1)}, u32[]{:S(2)}, u32[]{:S(2)}) collective-permute-start(f32[128,2,1]{0,1,2:T(2,128)S(1)} %collective-permute-done.8), channel_id=1, source_target_pairs={{32,0},{64,32},{96,64},{128,96},{160,128},{192,160},{224,192},{256... | collective-permute-start | bytes 3080 | tf_op jit(solution)/shard_map/ppermute | solution.py:33
  413.8 7.8 %collective-permute-start.3 = (f32[128,2,1]{0,1,2:T(2,128)S(1)}, f32[128,2,1]{0,1,2:T(2,128)S(1)}, u32[]{:S(2)}, u32[]{:S(2)}) collective-permute-start(f32[128,2,1]{0,1,2:T(2,128)S(1)} %collective-permute-done.2), channel_id=1, source_target_pairs={{0,32},{32,64},{64,96},{96,128},{128,160},{160,192},{192,224},{224... | collective-permute-start | bytes 3080 | tf_op jit(solution)/shard_map/ppermute | solution.py:30
  416.4 7.1 %collective-permute-start.10 = (f32[128,2,1]{0,1,2:T(2,128)S(1)}, f32[128,2,1]{0,1,2:T(2,128)S(1)}, u32[]{:S(2)}, u32[]{:S(2)}) collective-permute-start(f32[128,2,1]{0,1,2:T(2,128)S(1)} %collective-permute-done.9), channel_id=1, source_target_pairs={{32,0},{64,32},{96,64},{128,96},{160,128},{192,160},{224,192},{256... | collective-permute-start | bytes 3080 | tf_op jit(solution)/shard_map/ppermute | solution.py:33
  421.5 7.1 %collective-permute-start.4 = (f32[128,2,1]{0,1,2:T(2,128)S(1)}, f32[128,2,1]{0,1,2:T(2,128)S(1)}, u32[]{:S(2)}, u32[]{:S(2)}) collective-permute-start(f32[128,2,1]{0,1,2:T(2,128)S(1)} %collective-permute-done.3), channel_id=1, source_target_pairs={{0,32},{32,64},{64,96},{96,128},{128,160},{160,192},{192,224},{224... | collective-permute-start | bytes 3080 | tf_op jit(solution)/shard_map/ppermute | solution.py:30
  423.5 7.1 %collective-permute-start.11 = (f32[128,2,1]{0,1,2:T(2,128)S(1)}, f32[128,2,1]{0,1,2:T(2,128)S(1)}, u32[]{:S(2)}, u32[]{:S(2)}) collective-permute-start(f32[128,2,1]{0,1,2:T(2,128)S(1)} %collective-permute-done.10), channel_id=1, source_target_pairs={{32,0},{64,32},{96,64},{128,96},{160,128},{192,160},{224,192},{256... | collective-permute-start | bytes 3080 | tf_op jit(solution)/shard_map/ppermute | solution.py:33
  428.6 7.1 %collective-permute-start.5 = (f32[128,2,1]{0,1,2:T(2,128)S(1)}, f32[128,2,1]{0,1,2:T(2,128)S(1)}, u32[]{:S(2)}, u32[]{:S(2)}) collective-permute-start(f32[128,2,1]{0,1,2:T(2,128)S(1)} %collective-permute-done.4), channel_id=1, source_target_pairs={{0,32},{32,64},{64,96},{96,128},{128,160},{160,192},{192,224},{224... | collective-permute-start | bytes 3080 | tf_op jit(solution)/shard_map/ppermute | solution.py:30
  430.6 7.8 %collective-permute-start.12 = (f32[128,2,1]{0,1,2:T(2,128)S(1)}, f32[128,2,1]{0,1,2:T(2,128)S(1)}, u32[]{:S(2)}, u32[]{:S(2)}) collective-permute-start(f32[128,2,1]{0,1,2:T(2,128)S(1)} %collective-permute-done.11), channel_id=1, source_target_pairs={{32,0},{64,32},{96,64},{128,96},{160,128},{192,160},{224,192},{256... | collective-permute-start | bytes 3080 | tf_op jit(solution)/shard_map/ppermute | solution.py:33
  435.8 7.8 %collective-permute-start.6 = (f32[128,2,1]{0,1,2:T(2,128)S(1)}, f32[128,2,1]{0,1,2:T(2,128)S(1)}, u32[]{:S(2)}, u32[]{:S(2)}) collective-permute-start(f32[128,2,1]{0,1,2:T(2,128)S(1)} %collective-permute-done.5), channel_id=1, source_target_pairs={{0,32},{32,64},{64,96},{96,128},{128,160},{160,192},{192,224},{224... | collective-permute-start | bytes 3080 | tf_op jit(solution)/shard_map/ppermute | solution.py:30
  438.4 36.2 %collective-permute-start.13 = (f32[128,2,1]{0,1,2:T(2,128)S(1)}, f32[128,2,1]{0,1,2:T(2,128)S(1)}, u32[]{:S(2)}, u32[]{:S(2)}) collective-permute-start(f32[128,2,1]{0,1,2:T(2,128)S(1)} %collective-permute-done.12), channel_id=1, source_target_pairs={{32,0},{64,32},{96,64},{128,96},{160,128},{192,160},{224,192},{256... | collective-permute-start | bytes 3080 | tf_op jit(solution)/shard_map/ppermute | solution.py:33
  443.5 33.0 %collective-permute-start.7 = (f32[128,2,1]{0,1,2:T(2,128)S(1)}, f32[128,2,1]{0,1,2:T(2,128)S(1)}, u32[]{:S(2)}, u32[]{:S(2)}) collective-permute-start(f32[128,2,1]{0,1,2:T(2,128)S(1)} %collective-permute-done.6), channel_id=1, source_target_pairs={{0,32},{32,64},{64,96},{96,128},{128,160},{160,192},{192,224},{224... | collective-permute-start | bytes 3080 | tf_op jit(solution)/shard_map/ppermute | solution.py:30
  474.6 5.5 collective-permute-start.14
  484.8 3.2 copy-start.1
  488.5 3.6 copy-start.4
  492.6 1.0 copy-start.5
  494.1 3.2 copy-start.1
  497.8 3.6 copy-start.4
  501.9 1.0 copy-start.5
  503.4 3.2 copy-start.1
  507.1 3.6 copy-start.4
  511.3 1.0 copy-start.5
  512.8 3.2 copy-start.1
  516.5 3.6 copy-start.4
  520.6 1.0 copy-start.5
  521.6 8.9 %copy-start.6 = (f32[640,1,128]{0,2,1:T(8,128)S(1)}, f32[640,1,128]{0,2,1:T(8,128)}, u32[]{:S(2)}) copy-start(f32[640,1,128]{0,2,1:T(8,128)} %get-tuple-element.183) | copy-start | bytes 983044
  522.4 9.8 %all-to-all-start.2 = ((bf16[8,80,128]{2,1,0:T(8,128)(2,1)}), bf16[8,80,128]{2,1,0:T(8,128)(2,1)S(1)}, u32[]{:S(2)}, u32[]{:S(2)}) async-start(bf16[8,80,128]{2,1,0:T(8,128)(2,1)} %bitcast.48), calls=%async_computation.2 | async-start | bytes 327680 | tf_op jit(solution)/shard_map/all_to_all | solution.py:191
  527.2 139.4 %all-reduce.12.cloned.1.call-start = ((), (), s32[]{:S(2)}) async-start(), calls=%async_computation.9 | async-start | bytes 2097152
  532.2 9.8 %all-to-all-start.3 = ((bf16[8,80,128]{2,1,0:T(8,128)(2,1)}), bf16[8,80,128]{2,1,0:T(8,128)(2,1)S(1)}, u32[]{:S(2)}, u32[]{:S(2)}) async-start(bf16[8,80,128]{2,1,0:T(8,128)(2,1)} %bitcast.50), calls=%async_computation.3 | async-start | bytes 327680 | tf_op jit(solution)/shard_map/all_to_all | solution.py:198
  554.8 6.6 collective-permute-start.15
  556.3 5.3 collective-permute-start.16
Sparse Core Ops, SparseCore 0:
  10.7 75.5 all-gather.3
  179.8 66.8 reduce-scatter.7
  249.1 141.9 all-reduce.9
  416.5 67.7 all-gather.5
  530.6 135.9 all-reduce.11
